TPU v7x, 128 devices: a whole 4x4x4 slice. The times are simulated.
128 devices in a mesh: row: 8 (over z, x_hi), col: 16 (over x_lo, y, core).
Axes of the slice: x: 4 (x_hi: 2, x_lo: 2; x = x_hi * 2 + x_lo), y: 4, z: 4, core: 2. Of those that a mesh axis runs over, the one named last changes fastest.
Arguments:
- activations: bfloat16 [65536, 4096], P(('row', 'col')), may hold values from -6 to 6
- out_grads: bfloat16 [65536, 14336], P(('row', 'col')), may hold values from -6 to 6
- token_counts: int32 [128, 64], P(('row', 'col')), may hold values from 1 to 16, 512 in all within a row
- proj_seeds: int32 [2], replicated, may hold values from 0 to 29999
Outputs:
- kernel: float32 [8192, 8192], P('row', 'col')
Inputs may be any that keep to these rules, and one draw needn't show every extreme that they name: `token_counts`: each row sums to 512.
All inputs are finite; a program needn't handle non-finite values.
Results may differ from a plain program's by a relative error of at most 0.0025.
Values may be sent and summed in bfloat16 or wider, within the bound.
A program may use at most 192 MiB of HBM per device.

v0:
```python
import math

import jax
import jax.numpy as jnp
from jax import lax
from jax.sharding import PartitionSpec as P

KO = 128
KI = 64


modulus = 32749


def spread(array, axis, root):
    mine = lax.axis_index(axis) == root
    return lax.psum(jnp.where(mine, array, jnp.zeros_like(array)), axis)


def sign_table(table_rows, table_cols, seed_value):
    row_ids = lax.broadcasted_iota(jnp.int32, (table_rows, table_cols), 0)
    col_ids = lax.broadcasted_iota(jnp.int32, (table_rows, table_cols), 1)
    mixed_hash = (row_ids * 181 + col_ids * 7 + seed_value) % modulus
    mixed_hash = (mixed_hash * mixed_hash + 5471) % modulus
    mixed_hash = (mixed_hash * mixed_hash + col_ids * 31 + row_ids) % modulus
    mixed_hash = (mixed_hash * mixed_hash + 12007) % modulus
    return (1 - 2 * (mixed_hash % 2)).astype(jnp.bfloat16)


def projections(activations, out_grads, proj_seeds):
    in_signs = sign_table(activations.shape[1], KI, proj_seeds[0])
    out_signs = sign_table(out_grads.shape[1], KO, proj_seeds[1])
    grad_proj = jnp.dot(out_grads, out_signs, preferred_element_type=jnp.float32) * (
        1.0 / math.sqrt(out_grads.shape[1])
    )
    act_proj = jnp.dot(activations, in_signs, preferred_element_type=jnp.float32) * (
        1.0 / math.sqrt(activations.shape[1])
    )
    return (grad_proj, act_proj)


def local_features(grad_proj, act_proj, counts):
    tokens = grad_proj.shape[0]
    outer_terms = (grad_proj[:, :, None] * act_proj[:, None, :]).reshape(tokens, KO * KI)
    end_marks = jnp.cumsum(counts, dtype=jnp.int32)
    starts = end_marks - counts
    places = lax.broadcasted_iota(jnp.int32, (counts.shape[0], tokens), 1)
    member = ((places >= starts[:, None]) & (places < end_marks[:, None])).astype(jnp.float32)
    summed = jnp.dot(
        member, outer_terms, precision=lax.Precision.HIGHEST, preferred_element_type=jnp.float32
    )
    return summed.astype(jnp.bfloat16)


def cross_product(left_rows, right_rows):
    return lax.dot_general(
        left_rows, right_rows, (((1,), (1,)), ((), ())), preferred_element_type=jnp.float32
    )


def body(activations, out_grads, token_counts, proj_seeds):
    grad_proj, act_proj = projections(activations, out_grads, proj_seeds)
    kernel_scale = 1.0 / (KO * KI)
    local_count = token_counts.shape[1]
    panel_ratio = lax.axis_size("col") // lax.axis_size("row")
    panel_span = local_count * lax.axis_size("row")
    offset = lax.axis_index("col") % panel_ratio * panel_span
    source = lax.axis_index("col") // panel_ratio
    features = local_features(grad_proj, act_proj, token_counts[0])
    panel_rows = lax.all_gather(features, "col", axis=0, tiled=True)
    own_part = lax.dynamic_slice_in_dim(panel_rows, offset, panel_span, 0)
    panel_cols = spread(own_part, "row", source)
    kernel = cross_product(panel_rows, panel_cols)
    return kernel * kernel_scale


def solution(mesh):
    return jax.shard_map(
        body,
        mesh=mesh,
        in_specs=(P(("row", "col"), None), P(("row", "col"), None), P(("row", "col"), None), P()),
        out_specs=P("row", "col"),
        check_vma=False,
    )
```

profile of v0, /device:TPU:1, one launch (start us, length us, event | category | flops | bytes accessed | tf_op | source)
XLA Modules:
  0.0 543.2 jit_solution(16557143236162868196)
XLA Ops:
  6.5 0.0 all-gather.2.cloned.1.call-start
  6.6 1.3 fusion.80
  7.9 0.7 copy.8
  8.6 0.1 reduce-window.7
  8.7 0.1 reduce
  8.8 0.7 bitcast_subtract_fusion
  9.5 0.0 copy-start
  9.5 11.9 %fusion.52 = f32[512,64]{0,1:T(8,128)S(1)} fusion(bf16[512,4096]{1,0:T(8,128)(2,1)} %param.4, s32[64]{0:T(128)S(1)} %get-tuple-element.7, s32[]{:T(128)} %bitcast.4, s32[64]{0:T(128)S(1)} %get-tuple-element.8, s32[4096]{0:T(1024)S(1)} %iota_multiply_fusion.1), kind=kOutput, calls=%fused_computation.68 | convolution fusion | flops 280788992 | bytes 4342276 | tf_op jit(solution)/shard_map/dot_general | solution.py:36
  21.4 0.0 copy-done
  21.4 40.4 %fusion.49 = f32[512,128]{0,1:T(8,128)S(1)} fusion(bf16[512,14336]{1,0:T(8,128)(2,1)S(1)} %copy-done, s32[128]{0:T(128)S(1)} %get-tuple-element.9, s32[]{:T(128)} %bitcast.2, s32[128]{0:T(128)S(1)} %get-tuple-element.10, s32[14336]{0:T(1024)S(1)} %iota_multiply_fusion), kind=kOutput, calls=%fused_computation.66 | convolution fusion | flops 1965359104 | bytes 15000580 | tf_op jit(solution)/shard_map/dot_general | solution.py:33
  61.8 2.5 broadcast_multiply_fusion
  64.3 9.8 %convolution_convert_fusion = bf16[64,8192]{1,0:T(8,128)(2,1)} fusion(f32[512,8192]{0,1:T(8,128)S(1)} %bitcast.17, s32[64]{0:T(128)S(1)} %reduce, s32[64]{0:T(128)S(1)} %bitcast_subtract_fusion), kind=kOutput, calls=%fused_computation.7 | convolution fusion | flops 3221848064 | bytes 17826304 | tf_op jit(solution)/shard_map/dot_general | solution.py:49
  74.1 0.0 all-gather.2.cloned.1.call-update
  74.2 0.2 all-reduce.2.cloned.1.call-start
  74.4 95.1 %all-gather.2.cloned.1.call-done = bf16[1024,8192]{1,0:T(8,128)(2,1)} async-done(((bf16[64,8192]{1,0:T(8,128)(2,1)}), bf16[1024,8192]{1,0:T(8,128)(2,1)}) %all-gather.2.cloned.1.call-update) | async-done | bytes 16777232 | tf_op jit(solution)/shard_map/all_gather | solution.py:70
  169.6 8.7 %dynamic-slice_select_fusion = bf16[512,8192]{1,0:T(8,128)(2,1)} fusion(bf16[1024,8192]{1,0:T(8,128)(2,1)} %all-gather.2.cloned.1.call-done, s32[]{:T(128)S(6)} %select_n.79, pred[]{:T(512)S(6)} %eq.17), kind=kLoop, calls=%fused_computation.8 | loop fusion | flops 4194304 | bytes 16777220 | tf_op jit(solution)/shard_map/jit(_where)/select_n | solution.py:17
  178.2 0.0 all-reduce.2.cloned.1.call-update
  178.2 342.3 %all-reduce.2.cloned.1.call-done = bf16[512,8192]{1,0:T(8,128)(2,1)} async-done(((bf16[512,8192]{1,0:T(8,128)(2,1)}), bf16[512,8192]{1,0:T(8,128)(2,1)}) %all-reduce.2.cloned.1.call-update) | async-done | bytes 8388624 | tf_op jit(solution)/shard_map/psum | solution.py:17
  520.6 15.8 %convolution_multiply_fusion = f32[1024,512]{1,0:T(8,128)} fusion(bf16[1024,8192]{1,0:T(8,128)(2,1)} %all-gather.2.cloned.1.call-done, bf16[512,8192]{1,0:T(8,128)(2,1)} %all-reduce.2.cloned.1.call-done), kind=kOutput, calls=%fused_computation.64 | convolution fusion | flops 8590458880 | bytes 27262976 | tf_op jit(solution)/shard_map/dot_general | solution.py:56
  (4 shorter events, 0.0 us)
Async XLA Ops:
  6.5 163.0 %all-gather.2.cloned.1.call-start = ((), (), s32[]{:S(2)}) async-start(), calls=%async_computation | async-start | bytes 17825792 | tf_op jit(solution)/shard_map/all_gather | solution.py:70
  9.5 11.9 %copy-start = (bf16[512,14336]{1,0:T(8,128)(2,1)S(1)}, bf16[512,14336]{1,0:T(8,128)(2,1)}, u32[]{:S(2)}) copy-start(bf16[512,14336]{1,0:T(8,128)(2,1)} %param.5) | copy-start | bytes 44040196
  74.2 446.4 %all-reduce.2.cloned.1.call-start = ((), (), s32[]{:S(2)}) async-start(), calls=%async_computation.1 | async-start | bytes 16777216 | tf_op jit(solution)/shard_map/psum | solution.py:17
Sparse Core Ops, SparseCore 0:
  74.3 95.2 all-gather.1
  178.4 342.1 all-reduce.1
where the time goes:
time: 543 us
  waiting for transfers between devices  437 us (80%)
  matrix products  77.9 us (14%)
  between operations  13.5 us (2%)
  other arithmetic  12.1 us (2%)
    psum x1, waiting for transfers between devices, spread(): return lax.psum(jnp.where(mine, array, jnp.zeros_like(array)), axis)  342 us
    all_gather x1, waiting for transfers between devices, body(): panel_rows = lax.all_gather(features, 'col', axis=0, tiled=True)  95.1 us
    dot_general x1, matrix products, projections(): jnp.dot(out_grads, out_signs, preferred_element_type=jnp.float32)  40.4 us
    dot_general x1, matrix products, cross_product(): lax.dot_general(left_rows, right_rows, (((1,), (1,)), ((), ())), preferre...  15.8 us
    dot_general x1, matrix products, projections(): jnp.dot(activations, in_signs, preferred_element_type=jnp.float32)  11.9 us
  transfers between devices with their start and end apart: 2, of which 2 were waited for; matrix products, arithmetic and copies ran while one was open for 0% of the time, Pallas kernels for 0%

commit v1 on v0

v1 whole, which is shorter than its diff:
```python
import functools
import math

import jax
import jax.numpy as jnp
from jax import lax
from jax.experimental import pallas as pl
from jax.experimental.pallas import tpu as pltpu
from jax.sharding import PartitionSpec as P

KO = 128
KI = 64
MOD = 32749
MESH = pl.DeviceIdType.MESH
F32 = jnp.float32
I32 = jnp.int32
BF16 = jnp.bfloat16
I16 = jnp.int16

TOK = 512
EX = 64
STEPS = 16
ROWS_G = TOK
ROWS_A = ROWS_G + 4 * KI
ROWS = ROWS_A + 4 * 16
LANE = 128


def reduced(x):
    q = (x.astype(F32) * (1.0 / MOD)).astype(I32)
    return x - q * MOD


def signs_of(first, second):
    h = reduced(first * first + 5471)
    h = reduced(h * h + second)
    x = h * h + 12007
    q = (x.astype(F32) * (1.0 / MOD) + 0.5).astype(I32)
    r = x - q * MOD
    odd = (r ^ (r >> 31)) & 1
    return jnp.where(odd == 0, 1.0, -1.0).astype(F32).astype(BF16)


def centred(scalar):
    low = lax.rem(scalar, MOD)
    return jnp.where(low > MOD // 2, low - MOD, low)


def exponent(largest):
    return jnp.ceil(jnp.log2(jnp.maximum(largest, 1e-30)))


def project_kernel(seeds_ref, counts_ref, act_ref, grad_ref, out_ref, g_acc, a_acc, s_g, s_a):
    step = pl.program_id(0)
    depth_g = grad_ref.shape[1]
    depth_a = act_ref.shape[1]

    @pl.when(step == 0)
    def _():
        g_acc[...] = jnp.zeros_like(g_acc)
        a_acc[...] = jnp.zeros_like(a_acc)

    sub = lax.broadcasted_iota(I32, (LANE, KO), 0)
    lane = lax.broadcasted_iota(I32, (LANE, KO), 1)
    for part in range(depth_g // LANE):
        start = step * depth_g + part * LANE
        first = (181 * sub + 7 * lane) + centred(181 * start + seeds_ref[1])
        second = (sub + 31 * lane) + start
        s_g[part * LANE:(part + 1) * LANE, :] = signs_of(first, second)
    sub = lax.broadcasted_iota(I32, (KI, LANE), 0)
    lane = lax.broadcasted_iota(I32, (KI, LANE), 1)
    for part in range(depth_a // LANE):
        start = step * depth_a + part * LANE
        first = (181 * lane + 7 * sub) + centred(181 * start + seeds_ref[0])
        second = (lane + 31 * sub) + start
        s_a[:, part * LANE:(part + 1) * LANE] = signs_of(first, second)
    g_acc[...] += jnp.dot(grad_ref[...], s_g[...], preferred_element_type=F32)
    a_acc[...] += lax.dot_general(
        s_a[...], act_ref[...], (((1,), (1,)), ((), ())), preferred_element_type=F32
    )

    @pl.when(step == STEPS - 1)
    def _():
        g = g_acc[...]
        a = a_acc[...]
        size = jnp.abs(g)
        g_up = exponent(jnp.max(size, axis=1, keepdims=True))
        g_across = exponent(jnp.max(size.T, axis=0, keepdims=True))
        a_up = exponent(jnp.max(jnp.abs(a), axis=0, keepdims=True))
        out_ref[0:ROWS_G, :] = jnp.round(g * jnp.exp2(14.0 - g_up)).astype(I32).astype(I16)
        a = jnp.round(a * jnp.exp2(14.0 - a_up)).astype(I32).astype(I16)
        total = g_across + a_up
        places = lax.broadcasted_iota(I32, (1, TOK), 1)

        def tally(e, carry):
            end, owner = carry
            end = end + counts_ref[0, e]
            return end, owner + (places >= end).astype(I32)

        _, owner = lax.fori_loop(0, EX, tally, (jnp.int32(0), jnp.zeros((1, TOK), I32)))
        row = lax.broadcasted_iota(I32, (16, TOK), 0)
        facts = jnp.where(row == 0, total.astype(I32), jnp.where(row == 1, owner, 0)).astype(I16)
        for k in range(4):
            out_ref[ROWS_G + KI * k:ROWS_G + KI * (k + 1), :] = a[:, LANE * k:LANE * (k + 1)]
            out_ref[ROWS_A + 16 * k:ROWS_A + 16 * (k + 1), :] = facts[:, LANE * k:LANE * (k + 1)]


def project(activations, out_grads, counts, seeds):
    width_a = activations.shape[1] // STEPS
    width_g = out_grads.shape[1] // STEPS
    return pl.pallas_call(
        project_kernel,
        grid=(STEPS,),
        out_shape=jax.ShapeDtypeStruct((ROWS, LANE), I16),
        in_specs=[
            pl.BlockSpec(memory_space=pltpu.SMEM),
            pl.BlockSpec(memory_space=pltpu.SMEM),
            pl.BlockSpec((TOK, width_a), lambda s: (0, s)),
            pl.BlockSpec((TOK, width_g), lambda s: (0, s)),
        ],
        out_specs=pl.BlockSpec((ROWS, LANE), lambda s: (0, 0)),
        scratch_shapes=[
            pltpu.VMEM((TOK, KO), F32),
            pltpu.VMEM((KI, TOK), F32),
            pltpu.VMEM((width_g, KO), BF16),
            pltpu.VMEM((KI, width_a), BF16),
        ],
        compiler_params=pltpu.CompilerParams(vmem_limit_bytes=32 << 20),
        cost_estimate=pl.CostEstimate(flops=4 << 30, bytes_accessed=19 << 20, transcendentals=0),
        name="project",
    )(seeds, counts, activations, out_grads)


def form(held, slot, scale, target, row0, g_hi, g_lo, kin, a_work, hi_ref, lo_ref, lhs):
    g = held[slot, 0:ROWS_G, :].astype(I32).astype(F32)
    high = g.astype(BF16)
    g_hi[...] = high
    g_lo[...] = (g - high.astype(F32)).astype(BF16)
    for k in range(4):
        facts = held[slot, ROWS_A + 16 * k:ROWS_A + 16 * (k + 1), :].astype(I32)
        sizes = jnp.exp2(facts[0:1, :].astype(F32)) * scale
        part = held[slot, ROWS_G + KI * k:ROWS_G + KI * (k + 1), :].astype(I32).astype(F32)
        a_work[k, 0:KI, :] = part * sizes
        a_work[k, KI:KI + 8, :] = jnp.broadcast_to(facts[1:2, :].astype(F32), (8, LANE))
        kin[k] = jnp.broadcast_to((facts[1:2, :] >> 3).astype(F32), (LANE, LANE)).T.astype(BF16)
    sub = lax.broadcasted_iota(I32, (8, LANE), 0)

    def pair(p, carry):
        halves = []
        for half in range(2):
            group = 2 * p + half
            low = (group * 8).astype(F32)
            a = a_work[0]
            for k in range(1, 4):
                owner = a_work[k, KI:KI + 8, :]
                mine = ((owner >= low) & (owner < low + 8.0))[None]
                a = jnp.where(mine, a_work[k].reshape(KI // 8 + 1, 8, LANE), a.reshape(KI // 8 + 1, 8, LANE))
            a = a.reshape(KI + 8, LANE)
            member = a[KI:, :] == low + sub.astype(F32)
            a = a[:KI, :]
            hi = a.astype(BF16).astype(F32)
            hi_ref[half] = hi
            lo_ref[half] = a - hi
            for j in range(0, KI, 2):
                for k, ref in enumerate((hi_ref, lo_ref)):
                    rows = [
                        jnp.where(member, jnp.broadcast_to(ref[half, j + n:j + n + 1, :], (8, LANE)), 0.0)
                        for n in range(2)
                    ]
                    lhs[half, 8 * j:8 * j + 16, LANE * k:LANE * (k + 1)] = jnp.concatenate(rows, 0).astype(BF16)
            this = group.astype(F32).astype(BF16)
            above, below = g_hi[0:LANE, :], g_lo[0:LANE, :]
            for k in range(1, 4):
                mine = kin[k] == this
                above = jnp.where(mine, g_hi[LANE * k:LANE * (k + 1), :], above)
                below = jnp.where(mine, g_lo[LANE * k:LANE * (k + 1), :], below)
            weights = jnp.concatenate([above, below], axis=1)
            weights = jnp.concatenate([weights, weights], axis=0)
            both = jnp.dot(lhs[half], weights, preferred_element_type=F32)
            halves.append((both[:, :LANE] + both[:, LANE:]).reshape(KI, 8, LANE))
        features = jnp.concatenate(halves, axis=1).astype(BF16)
        at = pl.multiple_of(row0 + p * 16, 16)
        for j in range(KI):
            target[pl.ds(at, 16), LANE * j:LANE * (j + 1)] = features[j]
        return carry

    lax.fori_loop(0, 4, pair, 0)


def panel_kernel(n_row, n_col, packed_ref, out_ref, held, left, right,
                 g_hi, g_lo, kin, a_work, hi_ref, lo_ref, lhs, own_sem, send_row, send_col, arrive):
    r = lax.axis_index("row")
    c = lax.axis_index("col")
    span = n_col // n_row
    per = n_col // span
    panel = r * span + c // per
    home = c // span
    first = lax.rem(c, span) * per
    crossing = home != r

    barrier = pltpu.get_barrier_semaphore()
    for k in range(1, n_col):
        pl.semaphore_signal(barrier, inc=1, device_id=(r, lax.rem(c + k, n_col)), device_id_type=MESH)
    for k in range(1, n_row):
        pl.semaphore_signal(barrier, inc=1, device_id=(lax.rem(r + k, n_row), panel), device_id_type=MESH)

    @pl.when(crossing)
    def _():
        for k in range(per):
            pl.semaphore_signal(barrier, inc=1, device_id=(home, first + k), device_id_type=MESH)

    pl.semaphore_wait(barrier, n_col - 1 + n_row - 1 + jnp.where(crossing, per, 0))

    own = pltpu.make_async_copy(packed_ref, held.at[c], own_sem)
    own.start()

    def to_row(k):
        other = lax.rem(c + k, n_col)
        return pltpu.make_async_remote_copy(
            src_ref=packed_ref, dst_ref=held.at[c], send_sem=send_row.at[k - 1], recv_sem=arrive.at[c],
            device_id=(r, other), device_id_type=MESH)

    def to_col(k):
        slot = n_col + lax.rem(c, per)
        return pltpu.make_async_remote_copy(
            src_ref=packed_ref, dst_ref=held.at[slot], send_sem=send_col.at[k - 1], recv_sem=arrive.at[slot],
            device_id=(lax.rem(r + k, n_row), panel), device_id_type=MESH)

    for k in range(1, n_row):
        to_col(k).start()
    for k in range(1, n_col):
        to_row(k).start()

    work = (g_hi, g_lo, kin, a_work, hi_ref, lo_ref, lhs)
    unit = 2.0 ** -28 / 64.0
    scale = unit / math.sqrt(14336.0)

    def landed(slot):
        pltpu.make_async_remote_copy(
            src_ref=held.at[slot], dst_ref=held.at[slot], send_sem=own_sem, recv_sem=arrive.at[slot],
            device_id=(r, c), device_id_type=MESH).wait_recv()

    own.wait()
    form(held, c, scale / 64.0, left, c * EX, *work)

    def row_block(k, carry):
        slot = lax.rem(c + k, n_col)
        landed(slot)
        form(held, slot, scale / 64.0, left, slot * EX, *work)
        return carry

    lax.fori_loop(1, n_col, row_block, 0)

    def col_block(k, carry):
        @pl.when(crossing)
        def _():
            landed(n_col + k)

        slot = jnp.where(crossing, n_col + k, first + k)
        form(held, slot, scale / 128.0, right, k * EX, *work)
        return carry

    lax.fori_loop(0, per, col_block, 0)

    def tile(t, carry):
        at = pl.multiple_of(t * 256, 256)
        total = None
        for k in range(4):
            term = lax.dot_general(
                left[pl.ds(at, 256), 2048 * k:2048 * (k + 1)], right[:, 2048 * k:2048 * (k + 1)],
                (((1,), (1,)), ((), ())), preferred_element_type=F32)
            total = term if total is None else total + term
        out_ref[pl.ds(at, 256), :] = total
        return carry

    lax.fori_loop(0, 4, tile, 0)

    for k in range(1, n_row):
        to_col(k).wait_send()
    for k in range(1, n_col):
        to_row(k).wait_send()


def panels(packed, n_row, n_col):
    per = n_row
    rows, cols = n_col * EX, per * EX
    return pl.pallas_call(
        functools.partial(panel_kernel, n_row, n_col),
        out_shape=jax.ShapeDtypeStruct((rows, cols), F32),
        in_specs=[pl.BlockSpec(memory_space=pltpu.VMEM)],
        out_specs=pl.BlockSpec(memory_space=pltpu.VMEM),
        scratch_shapes=[
            pltpu.VMEM((n_col + per, ROWS, LANE), I16),
            pltpu.VMEM((rows, KO * KI), BF16),
            pltpu.VMEM((cols, KO * KI), BF16),
            pltpu.VMEM((TOK, KO), BF16),
            pltpu.VMEM((TOK, KO), BF16),
            pltpu.VMEM((4, LANE, LANE), BF16),
            pltpu.VMEM((4, KI + 8, LANE), F32),
            pltpu.VMEM((2, KI, LANE), F32),
            pltpu.VMEM((2, KI, LANE), F32),
            pltpu.VMEM((2, 8 * KI, 2 * LANE), BF16),
            pltpu.SemaphoreType.DMA,
            pltpu.SemaphoreType.DMA((n_col - 1,)),
            pltpu.SemaphoreType.DMA((n_row - 1,)),
            pltpu.SemaphoreType.DMA((n_col + per,)),
        ],
        compiler_params=pltpu.CompilerParams(
            collective_id=0, has_side_effects=True, vmem_limit_bytes=56 << 20),
        cost_estimate=pl.CostEstimate(flops=20 << 30, bytes_accessed=4 << 20, transcendentals=0),
        name="panels",
    )(packed)


def body(n_row, n_col, activations, out_grads, token_counts, proj_seeds):
    packed = project(activations, out_grads, token_counts, proj_seeds)
    return panels(packed, n_row, n_col)


def solution(mesh):
    return jax.shard_map(
        functools.partial(body, mesh.shape["row"], mesh.shape["col"]),
        mesh=mesh,
        in_specs=(P(("row", "col"), None), P(("row", "col"), None), P(("row", "col"), None), P()),
        out_specs=P("row", "col"),
        check_vma=False,
    )
```

time: 543 us -> 234 us (0.43)
  the two profiles are of different devices: /device:TPU:1 before, /device:TPU:83 now
where the time goes in v1:
time: 234 us; the launch traced here: 233 us
  Pallas kernels  221 us (94%)
  local copies, waits for them, and re-layouts  12.4 us (5%)
    pallas_call x1, Pallas kernels, panels(): pl.pallas_call(functools.partial(panel_kernel, n_row, n_col), out_shape=j...  203 us
    pallas_call x1, Pallas kernels, project(): pl.pallas_call(project_kernel, grid=(STEPS,), out_shape=jax.ShapeDtypeStr...  17.9 us
    unnamed x11, local copies, waits for them, and re-layouts  12.4 us

profile of v1, /device:TPU:83, one launch (start us, length us, event | category | flops | bytes accessed | tf_op | source)
XLA Modules:
  0.0 233.3 jit_solution(1177987830950989450)
XLA Ops:
  0.0 0.0 copy-start
  0.0 5.2 %copy-done = bf16[512,14336]{1,0:T(8,128)(2,1)S(1)} copy-done((bf16[512,14336]{1,0:T(8,128)(2,1)S(1)}, bf16[512,14336]{1,0:T(8,128)(2,1)}, u32[]{:S(2)}) %copy-start) | copy-done | bytes 14680088
  5.2 0.0 copy-start.1
  5.2 2.2 copy-done.1
  7.4 0.0 copy-start.3
  7.4 0.7 copy-done.3
  8.0 0.0 copy-start.4
  8.0 0.7 copy-done.4
  8.7 17.9 %project.1.packed_ref = s16[832,128]{1,0:T(8,128)(2,1)S(1)} custom-call(s32[2]{0:T(128)S(1)} %copy-done.3, s32[1,64]{1,0:T(1,128)S(1)} %copy-done.4, bf16[512,4096]{1,0:T(8,128)(2,1)S(1)} %copy-done.1, bf16[512,14336]{1,0:T(8,128)(2,1)S(1)} %copy-done), custom_call_target="tpu_custom_call" | custom-call | flops 4294967296 | bytes 19922944 | tf_op jit(solution)/shard_map/project/pallas_call | solution.py:111
  26.6 0.0 copy-start.2
  26.6 0.7 copy-done.2
  27.3 202.9 %panels.1 = f32[1024,512]{1,0:T(8,128)} custom-call(s16[832,128]{1,0:T(8,128)(2,1)} %copy-done.2), custom_call_target="tpu_custom_call" | custom-call | flops 21474836480 | bytes 4194304 | tf_op jit(solution)/shard_map/panels/pallas_call | solution.py:287
  230.2 3.1 %copy.6 = f32[1024,512]{1,0:T(8,128)} copy(f32[1024,512]{1,0:T(8,128)} %panels.1) | data formatting | bytes 4194304
Async XLA Ops:
  0.0 5.2 %copy-start = (bf16[512,14336]{1,0:T(8,128)(2,1)S(1)}, bf16[512,14336]{1,0:T(8,128)(2,1)}, u32[]{:S(2)}) copy-start(bf16[512,14336]{1,0:T(8,128)(2,1)} %grad_ref.1) | copy-start | bytes 44040196
  5.2 2.2 copy-start.1
  7.4 0.7 copy-start.3
  8.0 0.7 copy-start.4
  26.6 0.7 copy-start.2

commit v2 on v1

--- a/solution.py
+++ b/solution.py
@@ -125,7 +125,7 @@
             pltpu.VMEM((width_g, KO), BF16),
             pltpu.VMEM((KI, width_a), BF16),
         ],
-        compiler_params=pltpu.CompilerParams(vmem_limit_bytes=32 << 20),
+        compiler_params=pltpu.CompilerParams(vmem_limit_bytes=60 << 20),
         cost_estimate=pl.CostEstimate(flops=4 << 30, bytes_accessed=19 << 20, transcendentals=0),
         name="project",
     )(seeds, counts, activations, out_grads)
@@ -187,87 +187,153 @@
     lax.fori_loop(0, 4, pair, 0)
 
 
-def panel_kernel(n_row, n_col, packed_ref, out_ref, held, left, right,
-                 g_hi, g_lo, kin, a_work, hi_ref, lo_ref, lhs, own_sem, send_row, send_col, arrive):
-    r = lax.axis_index("row")
-    c = lax.axis_index("col")
-    span = n_col // n_row
-    per = n_col // span
-    panel = r * span + c // per
-    home = c // span
-    first = lax.rem(c, span) * per
-    crossing = home != r
+def panel_kernel(n_row, n_col, packed_ref, out_ref, held, panel, g_hi, g_lo, kin, a_work, hi_ref, lo_ref, lhs,
+                 send, arrive):
+    p = lax.axis_index("row")
+    core = lax.rem(lax.axis_index("col"), 2)
+    q = lax.axis_index("col") // 2
+    chips = n_col // 2
+    diagonal = p == q
+
+    def pair_q(m):
+        return lax.rem(m + 4, 8)
+
+    def ring_q(m, k):
+        return (m // 4) * 4 + lax.rem(m + k, 4)
+
+    def pair_p(m):
+        return m + 1 - 2 * lax.rem(m, 2)
+
+    def ring_p(m, k):
+        return lax.rem(m + 2 * k, 8)
+
+    sibling = (p, 2 * q + 1 - core)
+    flipped = (q, 2 * p + core)
+    row_pair, row_up, row_down = [(p, 2 * m + core) for m in (pair_q(q), ring_q(q, 1), ring_q(q, 3))]
+    col_pair, col_up, col_down = [(m, 2 * q + core) for m in (pair_p(p), ring_p(p, 1), ring_p(p, 3))]
 
     barrier = pltpu.get_barrier_semaphore()
-    for k in range(1, n_col):
-        pl.semaphore_signal(barrier, inc=1, device_id=(r, lax.rem(c + k, n_col)), device_id_type=MESH)
-    for k in range(1, n_row):
-        pl.semaphore_signal(barrier, inc=1, device_id=(lax.rem(r + k, n_row), panel), device_id_type=MESH)
-
-    @pl.when(crossing)
-    def _():
-        for k in range(per):
-            pl.semaphore_signal(barrier, inc=1, device_id=(home, first + k), device_id_type=MESH)
-
-    pl.semaphore_wait(barrier, n_col - 1 + n_row - 1 + jnp.where(crossing, per, 0))
-
-    own = pltpu.make_async_copy(packed_ref, held.at[c], own_sem)
+    for other in (sibling, row_pair, row_up, row_down, col_pair, col_up, col_down):
+        pl.semaphore_signal(barrier, inc=1, device_id=other, device_id_type=MESH)
+
+    @pl.when(jnp.logical_not(diagonal))
+    def _():
+        pl.semaphore_signal(barrier, inc=1, device_id=flipped, device_id_type=MESH)
+
+    pl.semaphore_wait(barrier, jnp.where(diagonal, 7, 8))
+
+    def row_slot(m):
+        return 2 * m + core
+
+    def col_slot(m):
+        return n_col + 2 * m + core
+
+    def copy(number, source, slot, device):
+        return pltpu.make_async_remote_copy(
+            src_ref=source, dst_ref=held.at[slot], send_sem=send.at[number], recv_sem=arrive.at[slot],
+            device_id=device, device_id_type=MESH)
+
+    def landed(slot):
+        copy(0, held.at[slot], slot, sibling).wait_recv()
+
+    own_slot = row_slot(q)
+    rows = [q, pair_q(q), ring_q(q, 3), ring_q(q, 1), pair_q(ring_q(q, 3)), pair_q(ring_q(q, 1)), ring_q(q, 2),
+            pair_q(ring_q(q, 2))]
+    cols = [p, pair_p(p), ring_p(p, 3), ring_p(p, 1), pair_p(ring_p(p, 3)), pair_p(ring_p(p, 1)), ring_p(p, 2),
+            pair_p(ring_p(p, 2))]
+    row_next = {0: (row_pair, row_up, row_down), 1: (row_up, row_down), 2: (row_up,), 5: (row_down,)}
+    col_next = {0: (col_pair, col_up, col_down), 1: (col_up, col_down), 2: (col_up,), 5: (col_down,)}
+
+    def row_sends(i):
+        slot = row_slot(rows[i])
+        source = packed_ref if i == 0 else held.at[slot]
+        base = 0 if i == 0 else sum(len(row_next.get(n, ())) + 1 for n in range(i))
+        return [copy(base + n, source, slot, device) for n, device in enumerate(row_next.get(i, ()) + (sibling,))]
+
+    def col_sends(i):
+        slot = col_slot(cols[i])
+        base = 16 + sum(len(col_next.get(n, ())) + 1 for n in range(i))
+        moves = [copy(base + n, held.at[slot], slot, device) for n, device in enumerate(col_next.get(i, ()))]
+        return moves, copy(base + len(moves), held.at[slot], slot, sibling), cols[i] // 4 != core
+
+    flip = pltpu.make_async_remote_copy(
+        src_ref=packed_ref, dst_ref=held.at[col_slot(q)], send_sem=send.at[15], recv_sem=arrive.at[col_slot(q)],
+        device_id=flipped, device_id_type=MESH)
+    stay = pltpu.make_async_copy(packed_ref, held.at[col_slot(q)], arrive.at[col_slot(q)])
+
+    @pl.when(jnp.logical_not(diagonal))
+    def _():
+        flip.start()
+
+    @pl.when(diagonal)
+    def _():
+        stay.start()
+
+    for move in row_sends(0):
+        move.start()
+    own = pltpu.make_async_copy(packed_ref, held.at[own_slot], arrive.at[own_slot])
     own.start()
 
-    def to_row(k):
-        other = lax.rem(c + k, n_col)
-        return pltpu.make_async_remote_copy(
-            src_ref=packed_ref, dst_ref=held.at[c], send_sem=send_row.at[k - 1], recv_sem=arrive.at[c],
-            device_id=(r, other), device_id_type=MESH)
-
-    def to_col(k):
-        slot = n_col + lax.rem(c, per)
-        return pltpu.make_async_remote_copy(
-            src_ref=packed_ref, dst_ref=held.at[slot], send_sem=send_col.at[k - 1], recv_sem=arrive.at[slot],
-            device_id=(lax.rem(r + k, n_row), panel), device_id_type=MESH)
-
-    for k in range(1, n_row):
-        to_col(k).start()
-    for k in range(1, n_col):
-        to_row(k).start()
-
-    work = (g_hi, g_lo, kin, a_work, hi_ref, lo_ref, lhs)
+    def row_step(i):
+        landed(row_slot(rows[i]))
+        if i > 0:
+            for move in row_sends(i):
+                move.start()
+
+    def col_step(i):
+        landed(col_slot(cols[i]))
+        moves, across, wanted = col_sends(i)
+        for move in moves:
+            move.start()
+
+        @pl.when(wanted)
+        def _():
+            across.start()
+
+    plan = {0: [(row_step, 0)], 2: [(row_step, 1), (col_step, 0)], 4: [(row_step, 2), (row_step, 3)],
+            6: [(col_step, 1), (row_step, 4), (row_step, 5)], 8: [(col_step, 2), (col_step, 3)],
+            10: [(row_step, 6)], 11: [(col_step, 5), (col_step, 4)], 12: [(row_step, 7)], 14: [(col_step, 6)],
+            16: [(col_step, 7)]}
     unit = 2.0 ** -28 / 64.0
     scale = unit / math.sqrt(14336.0)
 
-    def landed(slot):
-        pltpu.make_async_remote_copy(
-            src_ref=held.at[slot], dst_ref=held.at[slot], send_sem=own_sem, recv_sem=arrive.at[slot],
-            device_id=(r, c), device_id_type=MESH).wait_recv()
-
-    own.wait()
-    form(held, c, scale / 64.0, left, c * EX, *work)
-
-    def row_block(k, carry):
-        slot = lax.rem(c + k, n_col)
-        landed(slot)
-        form(held, slot, scale / 64.0, left, slot * EX, *work)
+    def pick(values, i):
+        value = values[0]
+        for n in range(1, len(values)):
+            value = jnp.where(i == n, values[n], value)
+        return value
+
+    def block(k, carry):
+        for at, steps in plan.items():
+            @pl.when(k == at)
+            def _():
+                for step, i in steps:
+                    step(i)
+
+        is_row = k < n_col
+        place = jnp.where(is_row, k, k - n_col) // 2
+        other = lax.rem(k, 2)
+        part = jnp.where(other == 0, core, 1 - core)
+        m = jnp.where(is_row, pick(rows, place), 4 * core + place)
+        slot = jnp.where(is_row, 0, n_col) + 2 * m + part
+
+        @pl.when(other == 1)
+        def _():
+            landed(slot)
+
+        row0 = jnp.where(is_row, slot, n_col + lax.rem(slot, 8)) * EX
+        form(held, slot, jnp.where(is_row, scale / 64.0, scale / 128.0), panel, row0,
+             g_hi, g_lo, kin, a_work, hi_ref, lo_ref, lhs)
         return carry
 
-    lax.fori_loop(1, n_col, row_block, 0)
-
-    def col_block(k, carry):
-        @pl.when(crossing)
-        def _():
-            landed(n_col + k)
-
-        slot = jnp.where(crossing, n_col + k, first + k)
-        form(held, slot, scale / 128.0, right, k * EX, *work)
-        return carry
-
-    lax.fori_loop(0, per, col_block, 0)
+    lax.fori_loop(0, n_col + 8, block, 0)
 
     def tile(t, carry):
         at = pl.multiple_of(t * 256, 256)
         total = None
         for k in range(4):
             term = lax.dot_general(
-                left[pl.ds(at, 256), 2048 * k:2048 * (k + 1)], right[:, 2048 * k:2048 * (k + 1)],
+                panel[pl.ds(at, 256), 2048 * k:2048 * (k + 1)], panel[n_col * EX:, 2048 * k:2048 * (k + 1)],
                 (((1,), (1,)), ((), ())), preferred_element_type=F32)
             total = term if total is None else total + term
         out_ref[pl.ds(at, 256), :] = total
@@ -275,10 +341,20 @@
 
     lax.fori_loop(0, 4, tile, 0)
 
-    for k in range(1, n_row):
-        to_col(k).wait_send()
-    for k in range(1, n_col):
-        to_row(k).wait_send()
+    @pl.when(jnp.logical_not(diagonal))
+    def _():
+        flip.wait_send()
+
+    for i in range(chips):
+        for move in row_sends(i):
+            move.wait_send()
+        moves, across, wanted = col_sends(i)
+        for move in moves:
+            move.wait_send()
+
+        @pl.when(wanted)
+        def _():
+            across.wait_send()
 
 
 def panels(packed, n_row, n_col):
@@ -290,9 +366,8 @@
         in_specs=[pl.BlockSpec(memory_space=pltpu.VMEM)],
         out_specs=pl.BlockSpec(memory_space=pltpu.VMEM),
         scratch_shapes=[
-            pltpu.VMEM((n_col + per, ROWS, LANE), I16),
-            pltpu.VMEM((rows, KO * KI), BF16),
-            pltpu.VMEM((cols, KO * KI), BF16),
+            pltpu.VMEM((2 * n_col, ROWS, LANE), I16),
+            pltpu.VMEM((rows + cols, KO * KI), BF16),
             pltpu.VMEM((TOK, KO), BF16),
             pltpu.VMEM((TOK, KO), BF16),
             pltpu.VMEM((4, LANE, LANE), BF16),
@@ -300,10 +375,8 @@
             pltpu.VMEM((2, KI, LANE), F32),
             pltpu.VMEM((2, KI, LANE), F32),
             pltpu.VMEM((2, 8 * KI, 2 * LANE), BF16),
-            pltpu.SemaphoreType.DMA,
-            pltpu.SemaphoreType.DMA((n_col - 1,)),
-            pltpu.SemaphoreType.DMA((n_row - 1,)),
-            pltpu.SemaphoreType.DMA((n_col + per,)),
+            pltpu.SemaphoreType.DMA((32,)),
+            pltpu.SemaphoreType.DMA((2 * n_col,)),
         ],
         compiler_params=pltpu.CompilerParams(
             collective_id=0, has_side_effects=True, vmem_limit_bytes=56 << 20),

time: 234 us -> 103 us (0.44)
  the two profiles are of different devices: /device:TPU:83 before, /device:TPU:6 now
where the time goes in v2:
time: 103 us
  Pallas kernels  99.8 us (97%)
  local copies, waits for them, and re-layouts  3.08 us (3%)
    pallas_call x1, Pallas kernels, panels(): pl.pallas_call(functools.partial(panel_kernel, n_row, n_col), out_shape=j...  79.6 us
    pallas_call x1, Pallas kernels, project(): pl.pallas_call(project_kernel, grid=(STEPS,), out_shape=jax.ShapeDtypeStr...  20.2 us
    unnamed x1, local copies, waits for them, and re-layouts  3.08 us

profile of v2, /device:TPU:6, one launch (start us, length us, event | category | flops | bytes accessed | tf_op | source)
XLA Modules:
  0.0 102.9 jit_solution(16659348779235966115)
XLA Ops:
  0.0 20.2 %project.1.packed_ref = s16[832,128]{1,0:T(8,128)(2,1)} custom-call(s32[2]{0:T(128)} %seeds_ref.1, s32[1,64]{1,0:T(1,128)} %counts_ref.1, bf16[512,4096]{1,0:T(8,128)(2,1)} %act_ref.1, bf16[512,14336]{1,0:T(8,128)(2,1)} %grad_ref.1), custom_call_target="tpu_custom_call" | custom-call | flops 4294967296 | bytes 19922944 | tf_op jit(solution)/shard_map/project/pallas_call | solution.py:111
  20.2 79.6 %panels.1 = f32[1024,512]{1,0:T(8,128)} custom-call(s16[832,128]{1,0:T(8,128)(2,1)} %project.1.packed_ref), custom_call_target="tpu_custom_call" | custom-call | flops 21474836480 | bytes 4194304 | tf_op jit(solution)/shard_map/panels/pallas_call | solution.py:363
  99.8 3.1 %copy.6 = f32[1024,512]{1,0:T(8,128)} copy(f32[1024,512]{1,0:T(8,128)} %panels.1) | data formatting | bytes 4194304

commit v3 on v2

--- a/solution.py
+++ b/solution.py
@@ -19,7 +19,8 @@
 
 TOK = 512
 EX = 64
-STEPS = 16
+STEPS = 7
+AHEAD = 2
 ROWS_G = TOK
 ROWS_A = ROWS_G + 4 * KI
 ROWS = ROWS_A + 4 * 16
@@ -50,80 +51,109 @@
     return jnp.ceil(jnp.log2(jnp.maximum(largest, 1e-30)))
 
 
-def project_kernel(seeds_ref, counts_ref, act_ref, grad_ref, out_ref, g_acc, a_acc, s_g, s_a):
-    step = pl.program_id(0)
-    depth_g = grad_ref.shape[1]
-    depth_a = act_ref.shape[1]
-
-    @pl.when(step == 0)
-    def _():
-        g_acc[...] = jnp.zeros_like(g_acc)
-        a_acc[...] = jnp.zeros_like(a_acc)
-
+def project_kernel(seeds_ref, counts_ref, act_hbm, grad_hbm, out_ref, act, grad, g_acc, a_acc, s_a, act_sem, grad_sem):
+    depth_g = grad.shape[1] // STEPS
+    depth_a = act.shape[1] // 8
+
+    def fetch_a(k):
+        span = pl.ds(k * (act.shape[1] // 4), act.shape[1] // 4)
+        return pltpu.make_async_copy(act_hbm.at[:, span], act.at[:, span], act_sem.at[k])
+
+    def fetch_g(k):
+        span = pl.ds(pl.multiple_of(k * depth_g, LANE), depth_g)
+        return pltpu.make_async_copy(grad_hbm.at[:, span], grad.at[:, span], grad_sem.at[k])
+
+    for k in range(AHEAD):
+        fetch_g(k).start()
+    g_acc[...] = jnp.zeros_like(g_acc)
+    sub_a = lax.broadcasted_iota(I32, (KI, LANE), 0)
+    lane_a = lax.broadcasted_iota(I32, (KI, LANE), 1)
+
+    def part_a(k, carry):
+        for part in range(depth_a // LANE):
+            start = k * depth_a + part * LANE
+            first = (181 * lane_a + 7 * sub_a) + centred(181 * start + seeds_ref[0])
+            second = (lane_a + 31 * sub_a) + start
+            s_a[:, pl.ds(pl.multiple_of(start, LANE), LANE)] = signs_of(first, second)
+        return carry
+
+    lax.fori_loop(0, 8, part_a, 0)
     sub = lax.broadcasted_iota(I32, (LANE, KO), 0)
     lane = lax.broadcasted_iota(I32, (LANE, KO), 1)
-    for part in range(depth_g // LANE):
-        start = step * depth_g + part * LANE
-        first = (181 * sub + 7 * lane) + centred(181 * start + seeds_ref[1])
-        second = (sub + 31 * lane) + start
-        s_g[part * LANE:(part + 1) * LANE, :] = signs_of(first, second)
-    sub = lax.broadcasted_iota(I32, (KI, LANE), 0)
-    lane = lax.broadcasted_iota(I32, (KI, LANE), 1)
-    for part in range(depth_a // LANE):
-        start = step * depth_a + part * LANE
-        first = (181 * lane + 7 * sub) + centred(181 * start + seeds_ref[0])
-        second = (lane + 31 * sub) + start
-        s_a[:, part * LANE:(part + 1) * LANE] = signs_of(first, second)
-    g_acc[...] += jnp.dot(grad_ref[...], s_g[...], preferred_element_type=F32)
-    a_acc[...] += lax.dot_general(
-        s_a[...], act_ref[...], (((1,), (1,)), ((), ())), preferred_element_type=F32
+
+    def part_g(k, carry):
+        fetch_g(k).wait()
+
+        @pl.when(k + AHEAD < STEPS)
+        def _():
+            fetch_g(k + AHEAD).start()
+
+        for n in range(4):
+            @pl.when(k == n + 1)
+            def _():
+                fetch_a(n).start()
+
+        signs = []
+        for part in range(depth_g // LANE):
+            start = k * depth_g + part * LANE
+            first = (181 * sub + 7 * lane) + centred(181 * start + seeds_ref[1])
+            second = (sub + 31 * lane) + start
+            signs.append(signs_of(first, second))
+        span = pl.ds(pl.multiple_of(k * depth_g, LANE), depth_g)
+        g_acc[...] += jnp.dot(grad[:, span], jnp.concatenate(signs, axis=0), preferred_element_type=F32)
+        return carry
+
+    lax.fori_loop(0, STEPS, part_g, 0)
+    for k in range(4):
+        fetch_a(k).wait()
+    a_acc[...] = lax.dot_general(
+        s_a[...], act[...], (((1,), (1,)), ((), ())), preferred_element_type=F32
     )
-
-    @pl.when(step == STEPS - 1)
-    def _():
-        g = g_acc[...]
-        a = a_acc[...]
-        size = jnp.abs(g)
-        g_up = exponent(jnp.max(size, axis=1, keepdims=True))
-        g_across = exponent(jnp.max(size.T, axis=0, keepdims=True))
-        a_up = exponent(jnp.max(jnp.abs(a), axis=0, keepdims=True))
-        out_ref[0:ROWS_G, :] = jnp.round(g * jnp.exp2(14.0 - g_up)).astype(I32).astype(I16)
-        a = jnp.round(a * jnp.exp2(14.0 - a_up)).astype(I32).astype(I16)
-        total = g_across + a_up
-        places = lax.broadcasted_iota(I32, (1, TOK), 1)
-
-        def tally(e, carry):
-            end, owner = carry
-            end = end + counts_ref[0, e]
-            return end, owner + (places >= end).astype(I32)
-
-        _, owner = lax.fori_loop(0, EX, tally, (jnp.int32(0), jnp.zeros((1, TOK), I32)))
-        row = lax.broadcasted_iota(I32, (16, TOK), 0)
-        facts = jnp.where(row == 0, total.astype(I32), jnp.where(row == 1, owner, 0)).astype(I16)
-        for k in range(4):
-            out_ref[ROWS_G + KI * k:ROWS_G + KI * (k + 1), :] = a[:, LANE * k:LANE * (k + 1)]
-            out_ref[ROWS_A + 16 * k:ROWS_A + 16 * (k + 1), :] = facts[:, LANE * k:LANE * (k + 1)]
+    g = g_acc[...]
+    a = a_acc[...]
+    size = jnp.abs(g)
+    g_up = exponent(jnp.max(size, axis=1, keepdims=True))
+    g_across = exponent(jnp.max(size.T, axis=0, keepdims=True))
+    a_up = exponent(jnp.max(jnp.abs(a), axis=0, keepdims=True))
+    out_ref[0:ROWS_G, :] = jnp.round(g * jnp.exp2(14.0 - g_up)).astype(I32).astype(I16)
+    a = jnp.round(a * jnp.exp2(14.0 - a_up)).astype(I32).astype(I16)
+    total = g_across + a_up
+    places = lax.broadcasted_iota(I32, (1, TOK), 1)
+
+    def tally(e, carry):
+        end, owner = carry
+        end = end + counts_ref[0, e]
+        return end, owner + (places >= end).astype(I32)
+
+    _, owner = lax.fori_loop(0, EX, tally, (jnp.int32(0), jnp.zeros((1, TOK), I32)))
+    row = lax.broadcasted_iota(I32, (16, TOK), 0)
+    facts = jnp.where(row == 0, total.astype(I32), jnp.where(row == 1, owner, 0)).astype(I16)
+    for k in range(4):
+        out_ref[ROWS_G + KI * k:ROWS_G + KI * (k + 1), :] = a[:, LANE * k:LANE * (k + 1)]
+        out_ref[ROWS_A + 16 * k:ROWS_A + 16 * (k + 1), :] = facts[:, LANE * k:LANE * (k + 1)]
 
 
 def project(activations, out_grads, counts, seeds):
-    width_a = activations.shape[1] // STEPS
-    width_g = out_grads.shape[1] // STEPS
+    depth_a = activations.shape[1]
+    depth_g = out_grads.shape[1]
     return pl.pallas_call(
         project_kernel,
-        grid=(STEPS,),
         out_shape=jax.ShapeDtypeStruct((ROWS, LANE), I16),
         in_specs=[
             pl.BlockSpec(memory_space=pltpu.SMEM),
             pl.BlockSpec(memory_space=pltpu.SMEM),
-            pl.BlockSpec((TOK, width_a), lambda s: (0, s)),
-            pl.BlockSpec((TOK, width_g), lambda s: (0, s)),
+            pl.BlockSpec(memory_space=pl.ANY),
+            pl.BlockSpec(memory_space=pl.ANY),
         ],
-        out_specs=pl.BlockSpec((ROWS, LANE), lambda s: (0, 0)),
+        out_specs=pl.BlockSpec(memory_space=pltpu.VMEM),
         scratch_shapes=[
+            pltpu.VMEM((TOK, depth_a), BF16),
+            pltpu.VMEM((TOK, depth_g), BF16),
             pltpu.VMEM((TOK, KO), F32),
             pltpu.VMEM((KI, TOK), F32),
-            pltpu.VMEM((width_g, KO), BF16),
-            pltpu.VMEM((KI, width_a), BF16),
+            pltpu.VMEM((KI, depth_a), BF16),
+            pltpu.SemaphoreType.DMA((4,)),
+            pltpu.SemaphoreType.DMA((STEPS,)),
         ],
         compiler_params=pltpu.CompilerParams(vmem_limit_bytes=60 << 20),
         cost_estimate=pl.CostEstimate(flops=4 << 30, bytes_accessed=19 << 20, transcendentals=0),
@@ -143,48 +173,42 @@
         a_work[k, 0:KI, :] = part * sizes
         a_work[k, KI:KI + 8, :] = jnp.broadcast_to(facts[1:2, :].astype(F32), (8, LANE))
         kin[k] = jnp.broadcast_to((facts[1:2, :] >> 3).astype(F32), (LANE, LANE)).T.astype(BF16)
-    sub = lax.broadcasted_iota(I32, (8, LANE), 0)
-
-    def pair(p, carry):
-        halves = []
-        for half in range(2):
-            group = 2 * p + half
-            low = (group * 8).astype(F32)
-            a = a_work[0]
-            for k in range(1, 4):
-                owner = a_work[k, KI:KI + 8, :]
-                mine = ((owner >= low) & (owner < low + 8.0))[None]
-                a = jnp.where(mine, a_work[k].reshape(KI // 8 + 1, 8, LANE), a.reshape(KI // 8 + 1, 8, LANE))
-            a = a.reshape(KI + 8, LANE)
-            member = a[KI:, :] == low + sub.astype(F32)
-            a = a[:KI, :]
-            hi = a.astype(BF16).astype(F32)
-            hi_ref[half] = hi
-            lo_ref[half] = a - hi
-            for j in range(0, KI, 2):
-                for k, ref in enumerate((hi_ref, lo_ref)):
-                    rows = [
-                        jnp.where(member, jnp.broadcast_to(ref[half, j + n:j + n + 1, :], (8, LANE)), 0.0)
-                        for n in range(2)
-                    ]
-                    lhs[half, 8 * j:8 * j + 16, LANE * k:LANE * (k + 1)] = jnp.concatenate(rows, 0).astype(BF16)
-            this = group.astype(F32).astype(BF16)
-            above, below = g_hi[0:LANE, :], g_lo[0:LANE, :]
-            for k in range(1, 4):
-                mine = kin[k] == this
-                above = jnp.where(mine, g_hi[LANE * k:LANE * (k + 1), :], above)
-                below = jnp.where(mine, g_lo[LANE * k:LANE * (k + 1), :], below)
-            weights = jnp.concatenate([above, below], axis=1)
-            weights = jnp.concatenate([weights, weights], axis=0)
-            both = jnp.dot(lhs[half], weights, preferred_element_type=F32)
-            halves.append((both[:, :LANE] + both[:, LANE:]).reshape(KI, 8, LANE))
-        features = jnp.concatenate(halves, axis=1).astype(BF16)
-        at = pl.multiple_of(row0 + p * 16, 16)
-        for j in range(KI):
-            target[pl.ds(at, 16), LANE * j:LANE * (j + 1)] = features[j]
-        return carry
-
-    lax.fori_loop(0, 4, pair, 0)
+    sub = lax.broadcasted_iota(I32, (16, LANE), 0) & 7
+    halves = []
+    for group in range(8):
+        low = 8 * group
+        near = max(low, LANE * (group - 4)) // LANE
+        far = (min(LANE * (group + 1), TOK - 8 * (7 - group)) - 1) // LANE
+        a = a_work[near].reshape(KI // 8 + 1, 8, LANE)
+        above, below = g_hi[LANE * near:LANE * (near + 1), :], g_lo[LANE * near:LANE * (near + 1), :]
+        for k in range(near + 1, far + 1):
+            owner = a_work[k, KI:KI + 8, :]
+            mine = ((owner >= float(low)) & (owner < float(low + 8)))[None]
+            a = jnp.where(mine, a_work[k].reshape(KI // 8 + 1, 8, LANE), a)
+            mine = kin[k] == jnp.bfloat16(group)
+            above = jnp.where(mine, g_hi[LANE * k:LANE * (k + 1), :], above)
+            below = jnp.where(mine, g_lo[LANE * k:LANE * (k + 1), :], below)
+        owner = jnp.concatenate([a[KI // 8]] * 2, axis=0)
+        member = jnp.where(owner == (sub + low).astype(F32), 1.0, 0.0).astype(BF16)
+        a = a[:KI // 8].reshape(KI, LANE)
+        hi = a.astype(BF16).astype(F32)
+        hi_ref[group] = hi
+        lo_ref[group] = a - hi
+        for j in range(0, KI, 2):
+            for k, ref in enumerate((hi_ref, lo_ref)):
+                rows = [jnp.broadcast_to(ref[group, j + n:j + n + 1, :], (8, LANE)) for n in range(2)]
+                tile = jnp.concatenate(rows, axis=0).astype(BF16) * member
+                lhs[group, 8 * j:8 * j + 16, LANE * k:LANE * (k + 1)] = tile
+        weights = jnp.concatenate([above, below], axis=1)
+        weights = jnp.concatenate([weights, weights], axis=0)
+        both = jnp.dot(lhs[group], weights, preferred_element_type=F32)
+        halves.append((both[:, :LANE] + both[:, LANE:]).reshape(KI, 8, LANE))
+        if group % 2 == 1:
+            features = jnp.concatenate(halves, axis=1).astype(BF16)
+            halves = []
+            at = pl.multiple_of(row0 + (group // 2) * 16, 16)
+            for j in range(KI):
+                target[pl.ds(at, 16), LANE * j:LANE * (j + 1)] = features[j]
 
 
 def panel_kernel(n_row, n_col, packed_ref, out_ref, held, panel, g_hi, g_lo, kin, a_work, hi_ref, lo_ref, lhs,
@@ -372,9 +396,9 @@
             pltpu.VMEM((TOK, KO), BF16),
             pltpu.VMEM((4, LANE, LANE), BF16),
             pltpu.VMEM((4, KI + 8, LANE), F32),
-            pltpu.VMEM((2, KI, LANE), F32),
-            pltpu.VMEM((2, KI, LANE), F32),
-            pltpu.VMEM((2, 8 * KI, 2 * LANE), BF16),
+            pltpu.VMEM((8, KI, LANE), F32),
+            pltpu.VMEM((8, KI, LANE), F32),
+            pltpu.VMEM((8, 8 * KI, 2 * LANE), BF16),
             pltpu.SemaphoreType.DMA((32,)),
             pltpu.SemaphoreType.DMA((2 * n_col,)),
         ],

time: 103 us -> 86.1 us (0.84)
  the two profiles are of different devices: /device:TPU:6 before, /device:TPU:2 now
where the time goes in v3:
time: 86.1 us; the launch traced here: 85.9 us
  Pallas kernels  82.8 us (96%)
  local copies, waits for them, and re-layouts  3.08 us (4%)
    pallas_call x1, Pallas kernels, panels(): pl.pallas_call(functools.partial(panel_kernel, n_row, n_col), out_shape=j...  66.1 us
    pallas_call x1, Pallas kernels, project(): pl.pallas_call(project_kernel, out_shape=jax.ShapeDtypeStruct((ROWS, LANE...  16.7 us
    unnamed x1, local copies, waits for them, and re-layouts  3.08 us

profile of v3, /device:TPU:2, one launch (start us, length us, event | category | flops | bytes accessed | tf_op | source)
XLA Modules:
  0.0 85.9 jit_solution(13344684090600008989)
XLA Ops:
  0.0 16.7 %project.1.packed_ref = s16[832,128]{1,0:T(8,128)(2,1)} custom-call(s32[2]{0:T(128)} %seeds_ref.1, s32[1,64]{1,0:T(1,128)} %counts_ref.1, bf16[512,4096]{1,0:T(8,128)(2,1)} %act_hbm.1, bf16[512,14336]{1,0:T(8,128)(2,1)} %grad_hbm.1), custom_call_target="tpu_custom_call" | custom-call | flops 4294967296 | bytes 19922944 | tf_op jit(solution)/shard_map/project/pallas_call | solution.py:139
  16.7 66.1 %panels.1 = f32[1024,512]{1,0:T(8,128)} custom-call(s16[832,128]{1,0:T(8,128)(2,1)} %project.1.packed_ref), custom_call_target="tpu_custom_call" | custom-call | flops 21474836480 | bytes 4194304 | tf_op jit(solution)/shard_map/panels/pallas_call | solution.py:387
  82.8 3.1 %copy.6 = f32[1024,512]{1,0:T(8,128)} copy(f32[1024,512]{1,0:T(8,128)} %panels.1) | data formatting | bytes 4194304

commit v4 on v3

--- a/solution.py
+++ b/solution.py
@@ -232,7 +232,17 @@
         return lax.rem(m + 2 * k, 8)
 
     sibling = (p, 2 * q + 1 - core)
-    flipped = (q, 2 * p + core)
+
+    def place_of(panel, j):
+        high = lax.rem(panel + j // 4 + panel // 4, 2)
+        return 2 * lax.rem(panel // 2 + j - panel + 8, 4) + high
+
+    def block_at(panel, m):
+        x_lo = lax.rem(panel // 4 + panel + m, 2)
+        return 4 * x_lo + lax.rem(m // 2 - panel // 2 + panel + 8, 4)
+
+    start_place = (place_of(p, q), 2 * p + core)
+    start_source = (q, 2 * block_at(q, p) + core)
     row_pair, row_up, row_down = [(p, 2 * m + core) for m in (pair_q(q), ring_q(q, 1), ring_q(q, 3))]
     col_pair, col_up, col_down = [(m, 2 * q + core) for m in (pair_p(p), ring_p(p, 1), ring_p(p, 3))]
 
@@ -242,7 +252,7 @@
 
     @pl.when(jnp.logical_not(diagonal))
     def _():
-        pl.semaphore_signal(barrier, inc=1, device_id=flipped, device_id_type=MESH)
+        pl.semaphore_signal(barrier, inc=1, device_id=start_source, device_id_type=MESH)
 
     pl.semaphore_wait(barrier, jnp.where(diagonal, 7, 8))
 
@@ -278,12 +288,11 @@
         slot = col_slot(cols[i])
         base = 16 + sum(len(col_next.get(n, ())) + 1 for n in range(i))
         moves = [copy(base + n, held.at[slot], slot, device) for n, device in enumerate(col_next.get(i, ()))]
-        return moves, copy(base + len(moves), held.at[slot], slot, sibling), cols[i] // 4 != core
-
-    flip = pltpu.make_async_remote_copy(
-        src_ref=packed_ref, dst_ref=held.at[col_slot(q)], send_sem=send.at[15], recv_sem=arrive.at[col_slot(q)],
-        device_id=flipped, device_id_type=MESH)
-    stay = pltpu.make_async_copy(packed_ref, held.at[col_slot(q)], arrive.at[col_slot(q)])
+        return moves, copy(base + len(moves), held.at[slot], slot, sibling), block_at(q, cols[i]) // 4 != core
+
+    first_slot = col_slot(place_of(p, q))
+    flip = copy(15, packed_ref, first_slot, start_place)
+    stay = pltpu.make_async_copy(packed_ref, held.at[first_slot], arrive.at[first_slot])
 
     @pl.when(jnp.logical_not(diagonal))
     def _():
@@ -314,10 +323,12 @@
         def _():
             across.start()
 
-    plan = {0: [(row_step, 0)], 2: [(row_step, 1), (col_step, 0)], 4: [(row_step, 2), (row_step, 3)],
-            6: [(col_step, 1), (row_step, 4), (row_step, 5)], 8: [(col_step, 2), (col_step, 3)],
-            10: [(row_step, 6)], 11: [(col_step, 5), (col_step, 4)], 12: [(row_step, 7)], 14: [(col_step, 6)],
-            16: [(col_step, 7)]}
+    plan = {0: [(row_step, 0)], 2: [(row_step, 1)], 3: [(col_step, 0)], 4: [(row_step, 2), (row_step, 3)],
+            6: [(row_step, 4), (row_step, 5)], 8: [(col_step, 1)], 9: [(col_step, 2), (col_step, 3)],
+            10: [(row_step, 6)], 12: [(row_step, 7)], 13: [(col_step, 5), (col_step, 4)], 15: [(col_step, 6)],
+            20: [(col_step, 7)]}
+    near = block_at(q, p) // 4 == core
+    wanted_places = [jnp.where(near, cols[a], cols[b]) for a, b in ((0, 1), (2, 4), (3, 5), (6, 7))]
     unit = 2.0 ** -28 / 64.0
     scale = unit / math.sqrt(14336.0)
 
@@ -327,7 +338,29 @@
             value = jnp.where(i == n, values[n], value)
         return value
 
+    def half(n):
+        low = n_col * EX + 256 * n
+        offsets = [pl.multiple_of(lax.rem(block_at(q, m), 4) * 128, 128) for m in wanted_places[2 * n:2 * n + 2]]
+
+        def tile(t, carry):
+            at = pl.multiple_of(t * 256, 256)
+            total = None
+            for k in range(4):
+                term = lax.dot_general(
+                    panel[pl.ds(at, 256), 2048 * k:2048 * (k + 1)], panel[low:low + 256, 2048 * k:2048 * (k + 1)],
+                    (((1,), (1,)), ((), ())), preferred_element_type=F32)
+                total = term if total is None else total + term
+            for i in range(2):
+                out_ref[pl.ds(at, 256), pl.ds(offsets[i], 128)] = total[:, 128 * i:128 * (i + 1)]
+            return carry
+
+        lax.fori_loop(0, 4, tile, 0)
+
     def block(k, carry):
+        @pl.when(k == n_col + 4)
+        def _():
+            half(0)
+
         for at, steps in plan.items():
             @pl.when(k == at)
             def _():
@@ -338,32 +371,20 @@
         place = jnp.where(is_row, k, k - n_col) // 2
         other = lax.rem(k, 2)
         part = jnp.where(other == 0, core, 1 - core)
-        m = jnp.where(is_row, pick(rows, place), 4 * core + place)
+        m = jnp.where(is_row, pick(rows, place), pick(wanted_places, place))
         slot = jnp.where(is_row, 0, n_col) + 2 * m + part
 
         @pl.when(other == 1)
         def _():
             landed(slot)
 
-        row0 = jnp.where(is_row, slot, n_col + lax.rem(slot, 8)) * EX
+        row0 = jnp.where(is_row, slot, n_col + 2 * place + part) * EX
         form(held, slot, jnp.where(is_row, scale / 64.0, scale / 128.0), panel, row0,
              g_hi, g_lo, kin, a_work, hi_ref, lo_ref, lhs)
         return carry
 
     lax.fori_loop(0, n_col + 8, block, 0)
-
-    def tile(t, carry):
-        at = pl.multiple_of(t * 256, 256)
-        total = None
-        for k in range(4):
-            term = lax.dot_general(
-                panel[pl.ds(at, 256), 2048 * k:2048 * (k + 1)], panel[n_col * EX:, 2048 * k:2048 * (k + 1)],
-                (((1,), (1,)), ((), ())), preferred_element_type=F32)
-            total = term if total is None else total + term
-        out_ref[pl.ds(at, 256), :] = total
-        return carry
-
-    lax.fori_loop(0, 4, tile, 0)
+    half(1)
 
     @pl.when(jnp.logical_not(diagonal))
     def _():

time: 86.1 us -> 85.4 us (level)
  the two profiles are of different devices: /device:TPU:2 before, /device:TPU:1 now
where the time goes in v4:
time: 85.4 us; the launch traced here: 84.7 us
  Pallas kernels  81.6 us (96%)
  local copies, waits for them, and re-layouts  3.08 us (4%)
    pallas_call x1, Pallas kernels, panels(): pl.pallas_call(functools.partial(panel_kernel, n_row, n_col), out_shape=j...  64.9 us
    pallas_call x1, Pallas kernels, project(): pl.pallas_call(project_kernel, out_shape=jax.ShapeDtypeStruct((ROWS, LANE...  16.7 us
    unnamed x1, local copies, waits for them, and re-layouts  3.08 us

profile of v4, /device:TPU:1, one launch (start us, length us, event | category | flops | bytes accessed | tf_op | source)
XLA Modules:
  0.0 84.7 jit_solution(17719929322312318741)
XLA Ops:
  0.0 16.7 %project.1.packed_ref = s16[832,128]{1,0:T(8,128)(2,1)} custom-call(s32[2]{0:T(128)} %seeds_ref.1, s32[1,64]{1,0:T(1,128)} %counts_ref.1, bf16[512,4096]{1,0:T(8,128)(2,1)} %act_hbm.1, bf16[512,14336]{1,0:T(8,128)(2,1)} %grad_hbm.1), custom_call_target="tpu_custom_call" | custom-call | flops 4294967296 | bytes 19922944 | tf_op jit(solution)/shard_map/project/pallas_call | solution.py:139
  16.7 64.9 %panels.1 = f32[1024,512]{1,0:T(8,128)} custom-call(s16[832,128]{1,0:T(8,128)(2,1)} %project.1.packed_ref), custom_call_target="tpu_custom_call" | custom-call | flops 21474836480 | bytes 4194304 | tf_op jit(solution)/shard_map/panels/pallas_call | solution.py:408
  81.6 3.1 %copy.6 = f32[1024,512]{1,0:T(8,128)} copy(f32[1024,512]{1,0:T(8,128)} %panels.1) | data formatting | bytes 4194304

commit v5 on v4

--- a/solution.py
+++ b/solution.py
@@ -23,7 +23,7 @@
 AHEAD = 2
 ROWS_G = TOK
 ROWS_A = ROWS_G + 4 * KI
-ROWS = ROWS_A + 4 * 16
+ROWS = ROWS_A + 16
 LANE = 128
 
 
@@ -126,11 +126,11 @@
         return end, owner + (places >= end).astype(I32)
 
     _, owner = lax.fori_loop(0, EX, tally, (jnp.int32(0), jnp.zeros((1, TOK), I32)))
-    row = lax.broadcasted_iota(I32, (16, TOK), 0)
-    facts = jnp.where(row == 0, total.astype(I32), jnp.where(row == 1, owner, 0)).astype(I16)
+    facts = [total.astype(I32)[:, LANE * k:LANE * (k + 1)] for k in range(4)]
+    facts += [owner[:, LANE * k:LANE * (k + 1)] for k in range(4)]
+    out_ref[ROWS_A:, :] = jnp.concatenate(facts + [jnp.zeros((8, LANE), I32)], axis=0).astype(I16)
     for k in range(4):
         out_ref[ROWS_G + KI * k:ROWS_G + KI * (k + 1), :] = a[:, LANE * k:LANE * (k + 1)]
-        out_ref[ROWS_A + 16 * k:ROWS_A + 16 * (k + 1), :] = facts[:, LANE * k:LANE * (k + 1)]
 
 
 def project(activations, out_grads, counts, seeds):
@@ -166,13 +166,14 @@
     high = g.astype(BF16)
     g_hi[...] = high
     g_lo[...] = (g - high.astype(F32)).astype(BF16)
+    facts = held[slot, ROWS_A:, :].astype(I32)
     for k in range(4):
-        facts = held[slot, ROWS_A + 16 * k:ROWS_A + 16 * (k + 1), :].astype(I32)
-        sizes = jnp.exp2(facts[0:1, :].astype(F32)) * scale
+        sizes = jnp.exp2(facts[k:k + 1, :].astype(F32)) * scale
+        owner = facts[4 + k:5 + k, :]
         part = held[slot, ROWS_G + KI * k:ROWS_G + KI * (k + 1), :].astype(I32).astype(F32)
         a_work[k, 0:KI, :] = part * sizes
-        a_work[k, KI:KI + 8, :] = jnp.broadcast_to(facts[1:2, :].astype(F32), (8, LANE))
-        kin[k] = jnp.broadcast_to((facts[1:2, :] >> 3).astype(F32), (LANE, LANE)).T.astype(BF16)
+        a_work[k, KI:KI + 8, :] = jnp.broadcast_to(owner.astype(F32), (8, LANE))
+        kin[k] = jnp.broadcast_to((owner >> 3).astype(F32), (LANE, LANE)).T.astype(BF16)
     sub = lax.broadcasted_iota(I32, (16, LANE), 0) & 7
     halves = []
     for group in range(8):
@@ -217,7 +218,6 @@
     core = lax.rem(lax.axis_index("col"), 2)
     q = lax.axis_index("col") // 2
     chips = n_col // 2
-    diagonal = p == q
 
     def pair_q(m):
         return lax.rem(m + 4, 8)
@@ -235,11 +235,11 @@
 
     def place_of(panel, j):
         high = lax.rem(panel + j // 4 + panel // 4, 2)
-        return 2 * lax.rem(panel // 2 + j - panel + 8, 4) + high
+        return 2 * lax.rem(panel // 2 + 2 + panel - j + 8, 4) + high
 
     def block_at(panel, m):
         x_lo = lax.rem(panel // 4 + panel + m, 2)
-        return 4 * x_lo + lax.rem(m // 2 - panel // 2 + panel + 8, 4)
+        return 4 * x_lo + lax.rem(panel + 2 + panel // 2 - m // 2 + 8, 4)
 
     start_place = (place_of(p, q), 2 * p + core)
     start_source = (q, 2 * block_at(q, p) + core)
@@ -250,11 +250,8 @@
     for other in (sibling, row_pair, row_up, row_down, col_pair, col_up, col_down):
         pl.semaphore_signal(barrier, inc=1, device_id=other, device_id_type=MESH)
 
-    @pl.when(jnp.logical_not(diagonal))
-    def _():
-        pl.semaphore_signal(barrier, inc=1, device_id=start_source, device_id_type=MESH)
-
-    pl.semaphore_wait(barrier, jnp.where(diagonal, 7, 8))
+    pl.semaphore_signal(barrier, inc=1, device_id=start_source, device_id_type=MESH)
+    pl.semaphore_wait(barrier, 8)
 
     def row_slot(m):
         return 2 * m + core
@@ -292,15 +289,7 @@
 
     first_slot = col_slot(place_of(p, q))
     flip = copy(15, packed_ref, first_slot, start_place)
-    stay = pltpu.make_async_copy(packed_ref, held.at[first_slot], arrive.at[first_slot])
-
-    @pl.when(jnp.logical_not(diagonal))
-    def _():
-        flip.start()
-
-    @pl.when(diagonal)
-    def _():
-        stay.start()
+    flip.start()
 
     for move in row_sends(0):
         move.start()
@@ -386,9 +375,7 @@
     lax.fori_loop(0, n_col + 8, block, 0)
     half(1)
 
-    @pl.when(jnp.logical_not(diagonal))
-    def _():
-        flip.wait_send()
+    flip.wait_send()
 
     for i in range(chips):
         for move in row_sends(i):

time: 85.4 us -> 83.9 us (0.982)
  Pallas kernels: 81.6 us -> 80.6 us
    pallas_call x1, Pallas kernels: 64.9 us -> 64 us  [panels(): pl.pallas_call(functools.partial(panel_kernel, n_row, n_col), out_shape=j...]
where the time goes in v5:
time: 83.9 us; the launch traced here: 83.7 us
  Pallas kernels  80.6 us (96%)
  local copies, waits for them, and re-layouts  3.08 us (4%)
    pallas_call x1, Pallas kernels, panels(): pl.pallas_call(functools.partial(panel_kernel, n_row, n_col), out_shape=j...  64 us
    pallas_call x1, Pallas kernels, project(): pl.pallas_call(project_kernel, out_shape=jax.ShapeDtypeStruct((ROWS, LANE...  16.7 us
    unnamed x1, local copies, waits for them, and re-layouts  3.08 us

profile of v5, /device:TPU:1, one launch (start us, length us, event | category | flops | bytes accessed | tf_op | source)
XLA Modules:
  0.0 83.7 jit_solution(12151149248982633957)
XLA Ops:
  0.0 16.7 %project.1.packed_ref = s16[784,128]{1,0:T(8,128)(2,1)} custom-call(s32[2]{0:T(128)} %seeds_ref.1, s32[1,64]{1,0:T(1,128)} %counts_ref.1, bf16[512,4096]{1,0:T(8,128)(2,1)} %act_hbm.1, bf16[512,14336]{1,0:T(8,128)(2,1)} %grad_hbm.1), custom_call_target="tpu_custom_call" | custom-call | flops 4294967296 | bytes 19922944 | tf_op jit(solution)/shard_map/project/pallas_call | solution.py:139
  16.7 64.0 %panels.1 = f32[1024,512]{1,0:T(8,128)} custom-call(s16[784,128]{1,0:T(8,128)(2,1)} %project.1.packed_ref), custom_call_target="tpu_custom_call" | custom-call | flops 21474836480 | bytes 4194304 | tf_op jit(solution)/shard_map/panels/pallas_call | solution.py:395
  80.7 3.1 %copy.6 = f32[1024,512]{1,0:T(8,128)} copy(f32[1024,512]{1,0:T(8,128)} %panels.1) | data formatting | bytes 4194304

commit v6 on v5

--- a/solution.py
+++ b/solution.py
@@ -394,7 +394,7 @@
     rows, cols = n_col * EX, per * EX
     return pl.pallas_call(
         functools.partial(panel_kernel, n_row, n_col),
-        out_shape=jax.ShapeDtypeStruct((rows, cols), F32),
+        out_shape=pltpu.VMEM((rows, cols), F32),
         in_specs=[pl.BlockSpec(memory_space=pltpu.VMEM)],
         out_specs=pl.BlockSpec(memory_space=pltpu.VMEM),
         scratch_shapes=[

time: 83.9 us -> 80.8 us (0.963)
  local copies, waits for them, and re-layouts: 3.08 us -> 1.32 us
  Pallas kernels: 80.6 us -> 79.3 us
    unnamed x1, local copies, waits for them, and re-layouts: 3.08 us -> 1.32 us
    pallas_call x1, Pallas kernels: 64 us -> 62.6 us  [panels(): pl.pallas_call(functools.partial(panel_kernel, n_row, n_col), out_shape=p...]
where the time goes in v6:
time: 80.8 us; the launch traced here: 80.6 us
  Pallas kernels  79.3 us (98%)
  local copies, waits for them, and re-layouts  1.32 us (2%)
    pallas_call x1, Pallas kernels, panels(): pl.pallas_call(functools.partial(panel_kernel, n_row, n_col), out_shape=p...  62.6 us
    pallas_call x1, Pallas kernels, project(): pl.pallas_call(project_kernel, out_shape=jax.ShapeDtypeStruct((ROWS, LANE...  16.7 us

profile of v6, /device:TPU:1, one launch (start us, length us, event | category | flops | bytes accessed | tf_op | source)
XLA Modules:
  0.0 80.6 jit_solution(4704089391705800477)
XLA Ops:
  0.0 16.7 %project.1.packed_ref = s16[784,128]{1,0:T(8,128)(2,1)} custom-call(s32[2]{0:T(128)} %seeds_ref.1, s32[1,64]{1,0:T(1,128)} %counts_ref.1, bf16[512,4096]{1,0:T(8,128)(2,1)} %act_hbm.1, bf16[512,14336]{1,0:T(8,128)(2,1)} %grad_hbm.1), custom_call_target="tpu_custom_call" | custom-call | flops 4294967296 | bytes 19922944 | tf_op jit(solution)/shard_map/project/pallas_call | solution.py:139
  16.7 62.6 %panels.1 = f32[1024,512]{1,0:T(8,128)S(1)} custom-call(s16[784,128]{1,0:T(8,128)(2,1)} %project.1.packed_ref), custom_call_target="tpu_custom_call" | custom-call | flops 21474836480 | bytes 4194304 | tf_op jit(solution)/shard_map/panels/pallas_call | solution.py:395
  79.3 1.3 %copy.6 = f32[1024,512]{1,0:T(8,128)} copy(f32[1024,512]{1,0:T(8,128)S(1)} %panels.1) | data formatting | bytes 4194304

commit v7 on v6

--- a/solution.py
+++ b/solution.py
@@ -43,7 +43,7 @@
 
 
 def centred(scalar):
-    low = lax.rem(scalar, MOD)
+    low = scalar - (((scalar >> 7) * 8196) >> 21) * MOD
     return jnp.where(low > MOD // 2, low - MOD, low)
 
 
@@ -77,6 +77,14 @@
             s_a[:, pl.ds(pl.multiple_of(start, LANE), LANE)] = signs_of(first, second)
         return carry
 
+    places = lax.broadcasted_iota(I32, (1, TOK), 1)
+
+    def tally(e, carry):
+        end, owner = carry
+        end = end + counts_ref[0, e]
+        return end, owner + (places >= end).astype(I32)
+
+    _, owner = lax.fori_loop(0, EX, tally, (jnp.int32(0), jnp.zeros((1, TOK), I32)))
     lax.fori_loop(0, 8, part_a, 0)
     sub = lax.broadcasted_iota(I32, (LANE, KO), 0)
     lane = lax.broadcasted_iota(I32, (LANE, KO), 1)
@@ -118,14 +126,6 @@
     out_ref[0:ROWS_G, :] = jnp.round(g * jnp.exp2(14.0 - g_up)).astype(I32).astype(I16)
     a = jnp.round(a * jnp.exp2(14.0 - a_up)).astype(I32).astype(I16)
     total = g_across + a_up
-    places = lax.broadcasted_iota(I32, (1, TOK), 1)
-
-    def tally(e, carry):
-        end, owner = carry
-        end = end + counts_ref[0, e]
-        return end, owner + (places >= end).astype(I32)
-
-    _, owner = lax.fori_loop(0, EX, tally, (jnp.int32(0), jnp.zeros((1, TOK), I32)))
     facts = [total.astype(I32)[:, LANE * k:LANE * (k + 1)] for k in range(4)]
     facts += [owner[:, LANE * k:LANE * (k + 1)] for k in range(4)]
     out_ref[ROWS_A:, :] = jnp.concatenate(facts + [jnp.zeros((8, LANE), I32)], axis=0).astype(I16)
@@ -395,7 +395,7 @@
     return pl.pallas_call(
         functools.partial(panel_kernel, n_row, n_col),
         out_shape=pltpu.VMEM((rows, cols), F32),
-        in_specs=[pl.BlockSpec(memory_space=pltpu.VMEM)],
+        in_specs=[pl.BlockSpec(memory_space=pl.ANY)],
         out_specs=pl.BlockSpec(memory_space=pltpu.VMEM),
         scratch_shapes=[
             pltpu.VMEM((2 * n_col, ROWS, LANE), I16),

time: 80.8 us -> 79.8 us (0.988)
  Pallas kernels: 79.3 us -> 78.3 us
where the time goes in v7:
time: 79.8 us; the launch traced here: 79.6 us
  Pallas kernels  78.3 us (98%)
  local copies, waits for them, and re-layouts  1.32 us (2%)
    pallas_call x1, Pallas kernels, panels(): pl.pallas_call(functools.partial(panel_kernel, n_row, n_col), out_shape=p...  61.9 us
    pallas_call x1, Pallas kernels, project(): pl.pallas_call(project_kernel, out_shape=jax.ShapeDtypeStruct((ROWS, LANE...  16.4 us

profile of v7, /device:TPU:1, one launch (start us, length us, event | category | flops | bytes accessed | tf_op | source)
XLA Modules:
  0.0 79.6 jit_solution(17497947617970149335)
XLA Ops:
  0.0 16.4 %project.1.packed_ref = s16[784,128]{1,0:T(8,128)(2,1)} custom-call(s32[2]{0:T(128)} %seeds_ref.1, s32[1,64]{1,0:T(1,128)} %counts_ref.1, bf16[512,4096]{1,0:T(8,128)(2,1)} %act_hbm.1, bf16[512,14336]{1,0:T(8,128)(2,1)} %grad_hbm.1), custom_call_target="tpu_custom_call" | custom-call | flops 4294967296 | bytes 19922944 | tf_op jit(solution)/shard_map/project/pallas_call | solution.py:139
  16.4 61.9 %panels.1 = f32[1024,512]{1,0:T(8,128)S(1)} custom-call(s16[784,128]{1,0:T(8,128)(2,1)} %project.1.packed_ref), custom_call_target="tpu_custom_call" | custom-call | flops 21474836480 | bytes 4194304 | tf_op jit(solution)/shard_map/panels/pallas_call | solution.py:395
  78.3 1.3 %copy.6 = f32[1024,512]{1,0:T(8,128)} copy(f32[1024,512]{1,0:T(8,128)S(1)} %panels.1) | data formatting | bytes 4194304

commit v8 on v7

--- a/solution.py
+++ b/solution.py
@@ -279,7 +279,7 @@
         slot = row_slot(rows[i])
         source = packed_ref if i == 0 else held.at[slot]
         base = 0 if i == 0 else sum(len(row_next.get(n, ())) + 1 for n in range(i))
-        return [copy(base + n, source, slot, device) for n, device in enumerate(row_next.get(i, ()) + (sibling,))]
+        return [copy(base + n, source, slot, device) for n, device in enumerate((sibling,) + row_next.get(i, ()))]
 
     def col_sends(i):
         slot = col_slot(cols[i])
@@ -289,12 +289,13 @@
 
     first_slot = col_slot(place_of(p, q))
     flip = copy(15, packed_ref, first_slot, start_place)
-    flip.start()
-
-    for move in row_sends(0):
-        move.start()
     own = pltpu.make_async_copy(packed_ref, held.at[own_slot], arrive.at[own_slot])
     own.start()
+    to_sibling, *to_others = row_sends(0)
+    to_sibling.start()
+    flip.start()
+    for move in to_others:
+        move.start()
 
     def row_step(i):
         landed(row_slot(rows[i]))
@@ -305,12 +306,13 @@
     def col_step(i):
         landed(col_slot(cols[i]))
         moves, across, wanted = col_sends(i)
-        for move in moves:
-            move.start()
 
         @pl.when(wanted)
         def _():
             across.start()
+
+        for move in moves:
+            move.start()
 
     plan = {0: [(row_step, 0)], 2: [(row_step, 1)], 3: [(col_step, 0)], 4: [(row_step, 2), (row_step, 3)],
             6: [(row_step, 4), (row_step, 5)], 8: [(col_step, 1)], 9: [(col_step, 2), (col_step, 3)],

time: 79.8 us -> 80 us (level)
  no operation moved by 1% of the time
where the time goes in v8:
time: 80 us; the launch traced here: 79.8 us
  Pallas kernels  78.5 us (98%)
  local copies, waits for them, and re-layouts  1.32 us (2%)
    pallas_call x1, Pallas kernels, panels(): pl.pallas_call(functools.partial(panel_kernel, n_row, n_col), out_shape=p...  62.1 us
    pallas_call x1, Pallas kernels, project(): pl.pallas_call(project_kernel, out_shape=jax.ShapeDtypeStruct((ROWS, LANE...  16.4 us

profile of v8, /device:TPU:1, one launch (start us, length us, event | category | flops | bytes accessed | tf_op | source)
XLA Modules:
  0.0 79.8 jit_solution(16496486519378933446)
XLA Ops:
  0.0 16.4 %project.1.packed_ref = s16[784,128]{1,0:T(8,128)(2,1)} custom-call(s32[2]{0:T(128)} %seeds_ref.1, s32[1,64]{1,0:T(1,128)} %counts_ref.1, bf16[512,4096]{1,0:T(8,128)(2,1)} %act_hbm.1, bf16[512,14336]{1,0:T(8,128)(2,1)} %grad_hbm.1), custom_call_target="tpu_custom_call" | custom-call | flops 4294967296 | bytes 19922944 | tf_op jit(solution)/shard_map/project/pallas_call | solution.py:139
  16.4 62.1 %panels.1 = f32[1024,512]{1,0:T(8,128)S(1)} custom-call(s16[784,128]{1,0:T(8,128)(2,1)} %project.1.packed_ref), custom_call_target="tpu_custom_call" | custom-call | flops 21474836480 | bytes 4194304 | tf_op jit(solution)/shard_map/panels/pallas_call | solution.py:397
  78.5 1.3 %copy.6 = f32[1024,512]{1,0:T(8,128)} copy(f32[1024,512]{1,0:T(8,128)S(1)} %panels.1) | data formatting | bytes 4194304

commit v9 on v7

--- a/solution.py
+++ b/solution.py
@@ -19,8 +19,8 @@
 
 TOK = 512
 EX = 64
-STEPS = 7
-AHEAD = 2
+STEPS = 4
+AHEAD = 1
 ROWS_G = TOK
 ROWS_A = ROWS_G + 4 * KI
 ROWS = ROWS_A + 16
@@ -97,7 +97,7 @@
             fetch_g(k + AHEAD).start()
 
         for n in range(4):
-            @pl.when(k == n + 1)
+            @pl.when(k == n)
             def _():
                 fetch_a(n).start()
 

time: 79.8 us -> 80.3 us (level)
  no operation moved by 1% of the time
where the time goes in v9:
time: 80.3 us; the launch traced here: 80.1 us
  Pallas kernels  78.8 us (98%)
  local copies, waits for them, and re-layouts  1.32 us (2%)
    pallas_call x1, Pallas kernels, panels(): pl.pallas_call(functools.partial(panel_kernel, n_row, n_col), out_shape=p...  61.9 us
    pallas_call x1, Pallas kernels, project(): pl.pallas_call(project_kernel, out_shape=jax.ShapeDtypeStruct((ROWS, LANE...  16.9 us

profile of v9, /device:TPU:1, one launch (start us, length us, event | category | flops | bytes accessed | tf_op | source)
XLA Modules:
  0.0 80.1 jit_solution(7491368140142129661)
XLA Ops:
  0.0 16.9 %project.1.packed_ref = s16[784,128]{1,0:T(8,128)(2,1)} custom-call(s32[2]{0:T(128)} %seeds_ref.1, s32[1,64]{1,0:T(1,128)} %counts_ref.1, bf16[512,4096]{1,0:T(8,128)(2,1)} %act_hbm.1, bf16[512,14336]{1,0:T(8,128)(2,1)} %grad_hbm.1), custom_call_target="tpu_custom_call" | custom-call | flops 4294967296 | bytes 19922944 | tf_op jit(solution)/shard_map/project/pallas_call | solution.py:139
  16.9 61.9 %panels.1 = f32[1024,512]{1,0:T(8,128)S(1)} custom-call(s16[784,128]{1,0:T(8,128)(2,1)} %project.1.packed_ref), custom_call_target="tpu_custom_call" | custom-call | flops 21474836480 | bytes 4194304 | tf_op jit(solution)/shard_map/panels/pallas_call | solution.py:395
  78.8 1.3 %copy.6 = f32[1024,512]{1,0:T(8,128)} copy(f32[1024,512]{1,0:T(8,128)S(1)} %panels.1) | data formatting | bytes 4194304
